TPU v7x, 32 devices: a whole 2x2x4 slice. The times are simulated.
32 devices in a mesh: parts: 2 (over x), store: 8 (over z, y), query: 2 (over core).
Axes of the slice: x: 2, y: 2, z: 4, core: 2. Of those that a mesh axis runs over, the one named last changes fastest.
Arguments:
- queries: bfloat16 [16, 768, 1024], P(('parts', 'store'), 'query'), parts along dimension 0, may hold values from -6 to 6
- store_blocks: bfloat16 [512, 128, 1024], P(('parts', 'store')), parts along dimension 0, may hold values from -6 to 6
- cand_owner: int32 [16, 112], P(('parts', 'store'), 'query'), parts along dimension 0, may hold values from 0 to 7, as said below
- cand_block: int32 [16, 112], P(('parts', 'store'), 'query'), parts along dimension 0, may hold values from 0 to 31
- pattern: int32 [16, 112, 6], P(('parts', 'store'), 'query'), parts along dimension 0, may hold values 0 or 1
- slot_index: int32 [16, 112], P(('parts', 'store'), 'query'), parts along dimension 0, may hold values from 0 to 31
Outputs:
- result: float32 [16, 32, 768], P(('parts', 'store'), None, 'query'), parts along dimension 0
There are 2 independent parts, one for each index of `parts`. A program takes and returns all parts, laid end to end along the dimension named above; each array names one. Nothing has to cross between parts.
Inputs may be any that keep to these rules, and one draw needn't show every extreme that they name: `cand_owner`: each tile's candidate list is 2 runs of 56 entries in order. Within one run no storage shard appears more than 10 times, and one shard appears exactly 10 times.
All inputs are finite; a program needn't handle non-finite values. No bound on the sum of `pattern` on one device may be relied on, other than what follows from the above.
Results may differ from a plain program's by a relative error of at most 0.0003.
Values may be sent and summed in bfloat16 or wider, within the bound.
A program may use at most 128 MiB of HBM per device.

v0:
```python
import math

import jax
import jax.numpy as jnp
from jax import lax
from jax.sharding import PartitionSpec as P

SUB = 128
SLOTS = 32


def inverse_scale(blocks):
    widened = blocks.astype(jnp.float32)
    squares = jnp.mean(widened * widened, axis=-1)
    return lax.rsqrt(squares + 1e-06) * (1.0 / math.sqrt(blocks.shape[-1]))


def slot_maxima(best_scores, mask_rows, slot_list, sub_rows):
    live_mask = jnp.repeat(mask_rows, sub_rows, axis=1) == 1
    slot_match = slot_list[:, None] == jnp.arange(SLOTS, dtype=jnp.int32)[None, :]
    masked = jnp.where(
        live_mask[:, None, :] & slot_match[:, :, None], best_scores[:, None, :], jnp.float32(0.0)
    )
    return jnp.max(masked, axis=0)


def placement_of(owner_list, capacity):
    list_length = owner_list.shape[0]
    order_ids = jnp.arange(list_length, dtype=jnp.int32)
    same_owner = owner_list[:, None] == owner_list[None, :]
    earlier = order_ids[:, None] > order_ids[None, :]
    owner_rank = jnp.sum((same_owner & earlier).astype(jnp.int32), axis=1)
    return owner_list * capacity + owner_rank


def request_table(position, local_list, total_slots):
    targets = jnp.arange(total_slots, dtype=jnp.int32)
    picked = jnp.where(position[None, :] == targets[:, None], local_list[None, :], 0)
    return jnp.sum(picked, axis=1)


def body(queries, store_blocks, cand_owner, cand_block, pattern, slot_index):
    owners = lax.axis_size("store")
    list_length = cand_owner.shape[1]
    capacity = max(2, 3 * list_length // (2 * owners))
    whole_tile = lax.all_gather(queries[0], "query", axis=0, tiled=True)
    position = placement_of(cand_owner[0], capacity)
    request_ids = request_table(position, cand_block[0], owners * capacity)
    asked_ids = lax.all_to_all(
        request_ids.reshape(owners, capacity), "store", split_axis=0, concat_axis=0, tiled=True
    )
    outgoing = store_blocks[asked_ids]
    received = lax.all_to_all(outgoing, "store", split_axis=0, concat_axis=0, tiled=True)
    products = jnp.einsum("qd,akvd->akqv", whole_tile, received, preferred_element_type=jnp.float32)
    slot_best = jnp.max(products * inverse_scale(received)[:, :, None, :], axis=-1)
    best_scores = slot_best.reshape(owners * capacity, slot_best.shape[-1])[position]
    merged = slot_maxima(best_scores, pattern[0], slot_index[0], SUB)
    core_pieces = lax.all_to_all(merged[None], "query", split_axis=2, concat_axis=0, tiled=True)
    return jnp.max(core_pieces, axis=0)[None]


def solution(mesh):
    placed = (
        P(("parts", "store"), "query", None),
        P(("parts", "store"), None, None),
        P(("parts", "store"), "query"),
        P(("parts", "store"), "query"),
        P(("parts", "store"), "query", None),
        P(("parts", "store"), "query"),
    )
    return jax.shard_map(
        body,
        mesh=mesh,
        in_specs=placed,
        out_specs=P(("parts", "store"), None, "query"),
        check_vma=False,
    )
```

profile of v0, /device:TPU:0, one launch (start us, length us, event | category | flops | bytes accessed | tf_op | source)
XLA Modules:
  0.0 540.5 jit_solution(7769389004080923109)
XLA Ops:
  6.5 0.9 convert_reduce_fusion
  7.4 0.7 fusion.3
  8.1 0.7 select_reduce_fusion.1
  8.9 0.1 all_to_all.20
  8.9 13.5 %all_to_all.29 = s32[8,1,10]{2,1,0:T(1,128)S(1)} all-to-all(s32[8,1,10]{2,1,0:T(1,128)S(1)} %bitcast.48), channel_id=1, replica_groups=mesh['parts'=2,'store'=8,'query'=2] {'store'}, dimensions={0} | all-to-all | bytes 640 | tf_op jit(solution)/shard_map/all_to_all | solution.py:49
  22.5 0.1 reshape.110
  22.6 12.3 %gather_fusion = bf16[80,128,1024]{2,1,0:T(8,128)(2,1)} fusion(bf16[32,128,1024]{2,1,0:T(8,128)(2,1)} %param.7, s32[1024]{0:T(1024)S(1)} %pad_clamp_fusion.1), kind=kCustom, calls=%fused_computation | custom fusion | bytes 41943360 | tf_op jit(solution)/shard_map/gather | solution.py:52
  34.9 6.2 %all-to-all-start.1 = ((bf16[8,10,128,1024]{3,2,1,0:T(8,128)(2,1)}), bf16[8,10,128,1024]{3,2,1,0:T(8,128)(2,1)}, u32[]{:S(2)}, u32[]{:S(2)}) async-start(bf16[8,10,128,1024]{3,2,1,0:T(8,128)(2,1)} %bitcast.40), calls=%async_computation.1 | async-start | bytes 41943040 | tf_op jit(solution)/shard_map/all_to_all | solution.py:53
  41.2 0.7 all-gather.3.cloned.1.call-update
  41.9 0.1 copy.19
  42.0 0.1 broadcast_in_dim.46
  42.3 450.3 %all-to-all-done.1 = bf16[8,10,128,1024]{3,2,1,0:T(8,128)(2,1)} async-done(((bf16[8,10,128,1024]{3,2,1,0:T(8,128)(2,1)}), bf16[8,10,128,1024]{3,2,1,0:T(8,128)(2,1)}, u32[]{:S(2)}, u32[]{:S(2)}) %all-to-all-start.1) | async-done | bytes 20971552 | tf_op jit(solution)/shard_map/all_to_all | solution.py:53
  492.6 8.8 %multiply_reduce_fusion = f32[8,10,128]{2,1,0:T(8,128)S(1)} fusion(bf16[8,10,128,1024]{3,2,1,0:T(8,128)(2,1)} %all-to-all-done.1), kind=kLoop, calls=%fused_computation.2 | loop fusion | flops 31447040 | bytes 21012480 | tf_op jit(solution)/shard_map/reduce_sum | solution.py:14
  501.6 21.4 %multiply_reduce_fusion.1 = f32[8,10,768]{2,1,0:T(8,128)S(1)} fusion(f32[8,10,128]{2,1,0:T(8,128)S(1)} %rsqrt_multiply_fusion, bf16[8,10,128,1024]{3,2,1,0:T(8,128)(2,1)} %all-to-all-done.1, bf16[1,768,1024]{2,1,0:T(8,128)(2,1)} %all-gather.3.cloned.1.call-done), kind=kOutput, calls=%fused_computation.3 | convolution fusion | flops 16121794560 | bytes 22831104 | tf_op jit(solution)/shard_map/qd,akvd->akqv/dot_general | solution.py:54
  523.0 0.7 gather_fusion.1
  523.6 1.2 select_reduce_fusion
  524.8 0.3 copy.16
  525.1 0.5 broadcast.84
  525.6 1.6 reduce.4
  527.3 0.2 reshape.127
  527.5 3.8 all_to_all.30
  531.3 0.9 reduce.5
  532.2 0.6 reshape.128
  532.9 0.7 copy.17
  (18 shorter events, 0.3 us)
Async XLA Ops:
  34.9 7.0 %copy-start = (s32[1,56,6]{1,0,2:T(1,128)S(1)}, s32[1,56,6]{1,0,2:T(1,128)}, u32[]{:S(2)}) copy-start(s32[1,56,6]{1,0,2:T(1,128)} %param.10) | copy-start | bytes 4036
  34.9 7.3 %copy-start.2 = (s32[1,56]{1,0:T(1,128)S(1)}, s32[1,56]{1,0:T(1,128)}, u32[]{:S(2)}) copy-start(s32[1,56]{1,0:T(1,128)} %param.8) | copy-start | bytes 676
  34.9 7.3 %copy-start.1 = (s32[1,56]{1,0:T(1,128)S(1)}, s32[1,56]{1,0:T(1,128)}, u32[]{:S(2)}) copy-start(s32[1,56]{1,0:T(1,128)} %param.11) | copy-start | bytes 676
  34.9 457.7 %all-to-all-start.1 = ((bf16[8,10,128,1024]{3,2,1,0:T(8,128)(2,1)}), bf16[8,10,128,1024]{3,2,1,0:T(8,128)(2,1)}, u32[]{:S(2)}, u32[]{:S(2)}) async-start(bf16[8,10,128,1024]{3,2,1,0:T(8,128)(2,1)} %bitcast.40), calls=%async_computation.1 | async-start | bytes 41943040 | tf_op jit(solution)/shard_map/all_to_all | solution.py:53
  41.1 460.4 %all-gather.3.cloned.1.call-start = ((), (), s32[]{:S(2)}) async-start(), calls=%async_computation.3 | async-start | bytes 2359296 | tf_op jit(solution)/shard_map/all_gather | solution.py:46
Sparse Core Ops, SparseCore 0:
  43.5 11.0 all-gather.2
where the time goes:
time: 541 us; the launch traced here: 540 us
  waiting for transfers between devices  451 us (83%)
  matrix products  21.4 us (4%)
  blocking collectives  17.3 us (3%)
  local copies, waits for them, and re-layouts  15.8 us (3%)
  other arithmetic  15 us (3%)
  between operations  13.6 us (3%)
  starting transfers between devices  6.26 us (1%)
    all_to_all x1, waiting for transfers between devices, body(): lax.all_to_all(outgoing, 'store', split_axis=0, concat_axis=0, tiled=True)  450 us
    dot_general x1, matrix products, body(): jnp.einsum('qd,akvd->akqv', whole_tile, received, preferred_element_type=...  21.4 us
    all_to_all x1, blocking collectives, body(): lax.all_to_all(request_ids.reshape(owners, capacity), 'store', split_axis...  13.5 us
    gather x1, local copies, waits for them, and re-layouts, body(): outgoing = store_blocks[asked_ids]  12.3 us
  transfers between devices with their start and end apart: 2, of which 1 were waited for; matrix products, arithmetic and copies ran while one was open for 2% of the time, Pallas kernels for 0%

commit v1 on v0

v1 whole, which is shorter than its diff:
```python
import functools
import math

import jax
import jax.numpy as jnp
from jax import lax
from jax.experimental import pallas as pl
from jax.experimental.pallas import tpu as pltpu
from jax.sharding import PartitionSpec as P

SUB = 128
SLOTS = 32
MIB = 1024 * 1024


def chunk_list(rows):
    last = rows // 6
    parts = [rows // 6, rows // 3, rows // 3, last]
    chunks, start = [], 0
    for size in parts:
        chunks.append((start, size))
        start += size
    assert start == rows
    return chunks


def kernel(
    n,
    group,
    q_hbm,
    blocks_hbm,
    owner_hbm,
    block_hbm,
    pattern_hbm,
    slot_hbm,
    out_ref,
    blocks,
    gathered,
    scale,
    best_out,
    best_in,
    owner_v,
    block_v,
    pattern_v,
    slot_v,
    owner_s,
    block_s,
    pattern_s,
    slot_s,
    local_sem,
    recv_sem,
    send_sem,
    best_recv,
    best_send,
    meta_recv,
    meta_send,
    smem_sem,
):
    ny = 2
    nz = n // ny
    rows = gathered.shape[1]
    stored, width, depth = blocks.shape
    chunks = chunk_list(rows)
    last = len(chunks) - 1
    me = lax.axis_index("store")
    core = lax.axis_index("query")
    y = lax.rem(me, ny)
    z = me // ny
    other_y = 1 - y
    UP, DOWN, ACROSS = 0, 1, 2

    load_blocks = pltpu.make_async_copy(blocks_hbm, blocks, local_sem.at[0])
    load_blocks.start()
    load_own = pltpu.make_async_copy(q_hbm.at[0], gathered.at[me], local_sem.at[1])
    load_own.start()

    barrier = pltpu.get_barrier_semaphore()

    @pl.loop(1, n)
    def _(step):
        pl.semaphore_signal(barrier, inc=1, device_id={"store": lax.rem(me + step, n)})

    pl.semaphore_signal(barrier, inc=1, device_id={"query": 1 - core})
    pl.semaphore_wait(barrier, n)

    targets = (
        jnp.minimum(z + 1, nz - 1) * ny + y,
        jnp.maximum(z - 1, 0) * ny + y,
        z * ny + other_y,
    )

    def copy_of(tile, c, way, own=False):
        start, size = chunks[c]
        held = gathered.at[tile, pl.ds(start, size)]
        return pltpu.make_async_remote_copy(
            src_ref=q_hbm.at[0, pl.ds(start, size)] if own else held,
            dst_ref=held,
            send_sem=send_sem.at[way, tile, c],
            recv_sem=recv_sem.at[tile, c],
            device_id={"store": targets[way]},
        )

    def wait_chunk(tile, c):
        copy_of(tile, c, ACROSS).wait_recv()

    for c in [last] + list(range(last)):
        copy_of(me, c, ACROSS, True).start()
    for c in range(last + 1):
        @pl.when(z > 0)
        def _():
            copy_of(me, c, DOWN, True).start()

        @pl.when(z < nz - 1)
        def _():
            copy_of(me, c, UP, True).start()

    metas = [
        pltpu.make_async_remote_copy(
            src_ref=src,
            dst_ref=dst,
            send_sem=meta_send.at[i],
            recv_sem=meta_recv.at[i],
            device_id={"query": 1 - core},
        )
        for i, (src, dst) in enumerate(
            [(owner_hbm, owner_v), (block_hbm, block_v), (pattern_hbm, pattern_v), (slot_hbm, slot_v)]
        )
    ]
    for copy in metas:
        copy.start()
    own_meta = [
        pltpu.make_async_copy(src, dst.at[0], smem_sem.at[i])
        for i, (src, dst) in enumerate(
            [(owner_hbm, owner_s), (block_hbm, block_s), (pattern_hbm, pattern_s), (slot_hbm, slot_s)]
        )
    ]
    for copy in own_meta:
        copy.start()

    load_blocks.wait()

    @pl.loop(0, stored)
    def _(b):
        wide = blocks[b].astype(jnp.float32)
        mean = jnp.sum(wide * wide, axis=1, keepdims=True) * (1.0 / depth)
        inverse = lax.rsqrt(mean + 1e-06) * (1.0 / math.sqrt(depth))
        scale[b] = jnp.broadcast_to(inverse, (width, SUB))

    def best_copy(tile):
        return pltpu.make_async_remote_copy(
            src_ref=best_out.at[tile],
            dst_ref=best_in.at[pl.ds(pl.multiple_of(me * stored, stored), stored)],
            send_sem=best_send.at[tile],
            recv_sem=best_recv.at[me],
            device_id={"store": tile},
        )

    def score(tile):
        @pl.loop(0, stored // group)
        def _(g):
            first = pl.multiple_of(g * group, group)
            picked = blocks[pl.ds(first, group)].reshape(group * width, depth)
            products = lax.dot_general(
                picked,
                gathered[tile],
                (((1,), (1,)), ((), ())),
                preferred_element_type=jnp.float32,
            ).reshape(group, width, rows)
            factor = scale[pl.ds(first, group)]
            for j in range(rows // SUB):
                piece = products[:, :, j * SUB : (j + 1) * SUB] * factor
                best_out[tile, pl.ds(first, group), j * SUB : (j + 1) * SUB] = jnp.max(piece, axis=1)

    def score_and_send(tile):
        score(tile)
        best_copy(tile).start()

    load_own.wait()
    score(me)
    best_in[pl.ds(pl.multiple_of(me * stored, stored), stored), :] = best_out[me]

    def pass_second(distance):
        above, below = z + distance, z - distance

        @pl.when(above < nz)
        def _():
            tile = above * ny + other_y
            wait_chunk(tile, last)

            @pl.when(z > 0)
            def _():
                copy_of(tile, last, DOWN).start()

        @pl.when(below >= 0)
        def _():
            tile = below * ny + other_y
            wait_chunk(tile, last)

            @pl.when(z < nz - 1)
            def _():
                copy_of(tile, last, UP).start()

    def finish_across(distance):
        for side in (1, -1):
            place = z + side * distance

            @pl.when((place >= 0) & (place < nz))
            def _():
                tile = place * ny + other_y
                for c in range(last):
                    wait_chunk(tile, c)
                score_and_send(tile)

    def pass_line(distance):
        above, below = z + distance, z - distance
        for c in range(last + 1):
            @pl.when(above < nz)
            def _():
                tile = above * ny + y
                wait_chunk(tile, c)

                @pl.when(z > 0)
                def _():
                    copy_of(tile, c, DOWN).start()

                if c < last:
                    copy_of(tile, c, ACROSS).start()

            @pl.when(below >= 0)
            def _():
                tile = below * ny + y
                wait_chunk(tile, c)

                @pl.when(z < nz - 1)
                def _():
                    copy_of(tile, c, UP).start()

                if c < last:
                    copy_of(tile, c, ACROSS).start()

    def score_line(distance):
        for side in (1, -1):
            place = z + side * distance

            @pl.when((place >= 0) & (place < nz))
            def _():
                score_and_send(place * ny + y)

    own_other = z * ny + other_y
    wait_chunk(own_other, last)

    @pl.when(z > 0)
    def _():
        copy_of(own_other, last, DOWN).start()

    @pl.when(z < nz - 1)
    def _():
        copy_of(own_other, last, UP).start()

    for c in range(last):
        wait_chunk(own_other, c)
    score_and_send(own_other)

    @pl.loop(1, nz)
    def _(distance):
        pass_line(distance)
        pass_second(distance)

        @pl.when(distance > 1)
        def _():
            finish_across(distance - 1)

        score_line(distance)

    finish_across(nz - 1)

    for copy in metas:
        copy.wait()
    for copy in own_meta:
        copy.wait()
    other_meta = [
        pltpu.make_async_copy(src, dst.at[1], smem_sem.at[i])
        for i, (src, dst) in enumerate(
            [(owner_v, owner_s), (block_v, block_s), (pattern_v, pattern_s), (slot_v, slot_s)]
        )
    ]
    for copy in other_meta:
        copy.start()
    for copy in other_meta:
        copy.wait()

    @pl.loop(1, n)
    def _(step):
        source = lax.rem(me + step, n)
        pltpu.make_async_remote_copy(
            src_ref=best_out.at[source],
            dst_ref=best_in.at[pl.ds(pl.multiple_of(source * stored, stored), stored)],
            send_sem=best_send.at[source],
            recv_sem=best_recv.at[source],
            device_id={"store": source},
        ).wait_recv()

    length = owner_s.shape[2]
    subs = rows // SUB
    slots = lax.broadcasted_iota(jnp.int32, (SLOTS, SUB), 0)

    def merge(c, totals):
        totals = list(totals)
        for run in range(2):
            source = owner_s[run, 0, c] * stored + block_s[run, 0, c]
            row = best_in[pl.ds(source, 1), :]
            slot = slot_s[run, 0, c]
            for j in range(subs):
                live = pattern_s[run, 0, c, core * subs + j] == 1
                wanted = jnp.where(live, slot, -1)
                piece = jnp.broadcast_to(row[:, j * SUB : (j + 1) * SUB], (SLOTS, SUB))
                totals[j] = jnp.maximum(totals[j], jnp.where(slots == wanted, piece, 0.0))
        return tuple(totals)

    zero = jnp.zeros((SLOTS, SUB), jnp.float32)
    totals = lax.fori_loop(0, length, merge, (zero,) * subs)
    for j in range(subs):
        out_ref[0, :, j * SUB : (j + 1) * SUB] = totals[j]

    for c in range(last + 1):
        copy_of(me, c, ACROSS, True).wait_send()

    @pl.loop(0, nz)
    def _(place):
        tile = place * ny + y
        across = place * ny + other_y

        @pl.when(place != z)
        def _():
            for c in range(last):
                copy_of(tile, c, ACROSS).wait_send()

        @pl.when((place <= z) & (z < nz - 1))
        def _():
            for c in range(last + 1):
                copy_of(tile, c, UP).wait_send()
            copy_of(across, last, UP).wait_send()

        @pl.when((place >= z) & (z > 0))
        def _():
            for c in range(last + 1):
                copy_of(tile, c, DOWN).wait_send()
            copy_of(across, last, DOWN).wait_send()

    @pl.loop(1, n)
    def _(step):
        best_copy(lax.rem(me + step, n)).wait_send()


def body(queries, store_blocks, cand_owner, cand_block, pattern, slot_index):
    n = lax.axis_size("store")
    rows, depth = queries.shape[1:]
    stored, width = store_blocks.shape[:2]
    length, subs = pattern.shape[1:]
    chunk_count = len(chunk_list(rows))
    flat = (1, length)
    return pl.pallas_call(
        functools.partial(kernel, n, 8),
        out_shape=jax.ShapeDtypeStruct((1, SLOTS, rows), jnp.float32),
        in_specs=[pl.BlockSpec(memory_space=pl.ANY)] * 6,
        out_specs=pl.BlockSpec(memory_space=pltpu.VMEM),
        scratch_shapes=[
            pltpu.VMEM((stored, width, depth), jnp.bfloat16),
            pltpu.VMEM((n, rows, depth), jnp.bfloat16),
            pltpu.VMEM((stored, width, SUB), jnp.float32),
            pltpu.VMEM((n, stored, rows), jnp.float32),
            pltpu.VMEM((n * stored, rows), jnp.float32),
            pltpu.VMEM(flat, jnp.int32),
            pltpu.VMEM(flat, jnp.int32),
            pltpu.VMEM((1, length, subs), jnp.int32),
            pltpu.VMEM(flat, jnp.int32),
            pltpu.SMEM((2,) + flat, jnp.int32),
            pltpu.SMEM((2,) + flat, jnp.int32),
            pltpu.SMEM((2, 1, length, subs), jnp.int32),
            pltpu.SMEM((2,) + flat, jnp.int32),
            pltpu.SemaphoreType.DMA((2,)),
            pltpu.SemaphoreType.DMA((n, chunk_count)),
            pltpu.SemaphoreType.DMA((3, n, chunk_count)),
            pltpu.SemaphoreType.DMA((n,)),
            pltpu.SemaphoreType.DMA((n,)),
            pltpu.SemaphoreType.DMA((4,)),
            pltpu.SemaphoreType.DMA((4,)),
            pltpu.SemaphoreType.DMA((4,)),
        ],
        compiler_params=pltpu.CompilerParams(
            collective_id=0, has_side_effects=True, vmem_limit_bytes=52 * MIB
        ),
        cost_estimate=pl.CostEstimate(
            flops=2 * n * rows * stored * width * depth,
            bytes_accessed=stored * width * depth * 2,
            transcendentals=0,
        ),
    )(queries, store_blocks, cand_owner, cand_block, pattern, slot_index)


def solution(mesh):
    placed = (
        P(("parts", "store"), "query", None),
        P(("parts", "store"), None, None),
        P(("parts", "store"), "query"),
        P(("parts", "store"), "query"),
        P(("parts", "store"), "query", None),
        P(("parts", "store"), "query"),
    )
    return jax.shard_map(
        body,
        mesh=mesh,
        in_specs=placed,
        out_specs=P(("parts", "store"), None, "query"),
        check_vma=False,
    )
```

time: 541 us -> 98.7 us (0.18)
  waiting for transfers between devices: 451 us -> 0 us
  Pallas kernels: 0 us -> 94 us
  matrix products: 21.4 us -> 0 us
  blocking collectives: 17.3 us -> 0 us
  other arithmetic: 15 us -> 0 us
  between operations: 13.6 us -> 0.01 us
  local copies, waits for them, and re-layouts: 15.8 us -> 4.49 us
  starting transfers between devices: 6.26 us -> 0 us
    all_to_all x1 -> x0, waiting for transfers between devices: 450 us -> none  [body(): lax.all_to_all(outgoing, 'store', split_axis=0, concat_axis=0, tiled=True)]
    pallas_call x0 -> x1, Pallas kernels: none -> 94 us  [body(): pl.pallas_call(functools.partial(kernel, n, 8), out_shape=jax.ShapeDtypeS...]
    dot_general x1 -> x0, matrix products: 21.4 us -> none  [body(): jnp.einsum('qd,akvd->akqv', whole_tile, received, preferred_element_type=...]
    all_to_all x2 -> x0, blocking collectives: 17.3 us -> none  [the longest x1 13.5 us: body(): lax.all_to_all(request_ids.reshape(owners, capacity), 'store', split_axis...]
    gather x2 -> x0, local copies, waits for them, and re-layouts: 13 us -> none  [the longest x1 12.3 us: body(): outgoing = store_blocks[asked_ids]]
    reduce_sum x3 -> x0, other arithmetic: 10.5 us -> none  [the longest x1 8.85 us: inverse_scale(): squares = jnp.mean(widened * widened, axis=-1)]
    all_to_all x1 -> x0, starting transfers between devices: 6.22 us -> none  [body(): lax.all_to_all(outgoing, 'store', split_axis=0, concat_axis=0, tiled=True)]
  transfers between devices with their start and end apart: 2 -> 0, of which waited for: 1 -> 0; matrix products, arithmetic and copies ran while one was open for 2% -> 0% of each run, Pallas kernels for 0% -> 0%
where the time goes in v1:
time: 98.7 us; the launch traced here: 98.5 us
  Pallas kernels  94 us (95%)
  local copies, waits for them, and re-layouts  4.49 us (5%)
    pallas_call x1, Pallas kernels, body(): pl.pallas_call(functools.partial(kernel, n, 8), out_shape=jax.ShapeDtypeS...  94 us
    unnamed x10, local copies, waits for them, and re-layouts  4.49 us

profile of v1, /device:TPU:0, one launch (start us, length us, event | category | flops | bytes accessed | tf_op | source)
XLA Modules:
  0.0 98.5 jit_solution(17421052007766068878)
XLA Ops:
  0.0 0.8 copy.7.pattern_hbm
  0.8 0.0 copy-start
  0.8 1.1 %copy-done = bf16[1,384,1024]{2,1,0:T(8,128)(2,1)S(1)} copy-done((bf16[1,384,1024]{2,1,0:T(8,128)(2,1)S(1)}, bf16[1,384,1024]{2,1,0:T(8,128)(2,1)}, u32[]{:S(2)}) %copy-start) | copy-done | bytes 786456
  1.9 0.0 copy-start.1
  1.9 0.7 copy-done.1
  2.6 0.0 copy-start.2
  2.6 0.7 copy-done.2
  3.2 0.0 copy-start.3
  3.2 0.7 copy-done.3
  3.9 94.0 %shard_map.64 = f32[1,32,384]{2,1,0:T(8,128)S(1)} custom-call(bf16[1,384,1024]{2,1,0:T(8,128)(2,1)S(1)} %copy-done, bf16[32,128,1024]{2,1,0:T(8,128)(2,1)} %blocks_hbm.1, s32[1,56]{1,0:T(1,128)S(1)} %copy-done.1, s32[1,56]{1,0:T(1,128)S(1)} %copy-done.2, s32[1,56,6]{2,1,0:T(8,128)S(1)} %copy.7.pattern_hbm, s32[1,56]{1,0:T(1,128)S(1)} %copy-done.3), custom_call_target="tpu_custom_call" | custom-call | flops 25769803776 | bytes 8388608 | tf_op jit(solution)/shard_map/pallas_call | solution.py:362
  97.9 0.6 copy.9
Async XLA Ops:
  0.8 1.1 %copy-start = (bf16[1,384,1024]{2,1,0:T(8,128)(2,1)S(1)}, bf16[1,384,1024]{2,1,0:T(8,128)(2,1)}, u32[]{:S(2)}) copy-start(bf16[1,384,1024]{2,1,0:T(8,128)(2,1)} %q_hbm.1) | copy-start | bytes 2359300
  1.9 0.7 copy-start.1
  2.6 0.7 copy-start.2
  3.2 0.7 copy-start.3

commit v2 on v1

v2 whole, which is shorter than its diff:
```python
import functools
import math

import jax
import jax.numpy as jnp
from jax import lax
from jax.experimental import pallas as pl
from jax.experimental.pallas import tpu as pltpu
from jax.sharding import PartitionSpec as P

SUB = 128
SLOTS = 32
MIB = 1024 * 1024


CHUNKS = 6
UNIT = 256


def kernel(
    n,
    group,
    q_hbm,
    blocks_hbm,
    owner_hbm,
    block_hbm,
    pattern_hbm,
    slot_hbm,
    out_ref,
    blocks,
    gathered,
    scale,
    best_out,
    best_in,
    owner_v,
    block_v,
    pattern_v,
    slot_v,
    owner_s,
    block_s,
    pattern_s,
    slot_s,
    local_sem,
    recv_sem,
    send_sem,
    best_recv,
    best_send,
    meta_recv,
    meta_send,
    smem_sem,
):
    ny = 2
    nz = n // ny
    rows = gathered.shape[0] // n
    piece_rows = rows // CHUNKS
    subs = rows // SUB
    stored, width, depth = blocks.shape
    last = CHUNKS - 1
    me = lax.axis_index("store")
    core = lax.axis_index("query")
    y = lax.rem(me, ny)
    z = me // ny
    other_y = 1 - y
    UP, DOWN, ACROSS = 0, 1, 2
    mine = z * ny

    def rows_of(slot, c, count=1):
        start = pl.multiple_of(slot * rows + c * piece_rows, piece_rows)
        return gathered.at[pl.ds(start, count * piece_rows)]

    load_blocks = pltpu.make_async_copy(blocks_hbm, blocks, local_sem.at[0])
    load_blocks.start()
    load_own = pltpu.make_async_copy(q_hbm.at[0], rows_of(mine, 0, CHUNKS), local_sem.at[1])
    load_own.start()

    barrier = pltpu.get_barrier_semaphore()

    @pl.loop(1, n)
    def _(step):
        pl.semaphore_signal(barrier, inc=1, device_id={"store": lax.rem(me + step, n)})

    pl.semaphore_signal(barrier, inc=1, device_id={"query": 1 - core})
    pl.semaphore_wait(barrier, n)

    targets = (
        jnp.minimum(z + 1, nz - 1) * ny + y,
        jnp.maximum(z - 1, 0) * ny + y,
        z * ny + other_y,
    )

    def copy_of(slot, c, way, own=False):
        source = q_hbm.at[0, pl.ds(c * piece_rows, piece_rows)] if own else rows_of(slot, c)
        landing = slot + 1 if way == ACROSS else slot
        return pltpu.make_async_remote_copy(
            src_ref=source,
            dst_ref=rows_of(landing, c),
            send_sem=send_sem.at[way, slot, c],
            recv_sem=recv_sem.at[landing, c],
            device_id={"store": targets[way]},
        )

    def wait_chunk(slot, c):
        copy_of(slot, c, UP).wait_recv()

    for c in [last] + list(range(last)):
        copy_of(mine, c, ACROSS, True).start()
    for c in range(last + 1):
        @pl.when(z > 0)
        def _():
            copy_of(mine, c, DOWN, True).start()

        @pl.when(z < nz - 1)
        def _():
            copy_of(mine, c, UP, True).start()

    metas = [
        pltpu.make_async_remote_copy(
            src_ref=src,
            dst_ref=dst,
            send_sem=meta_send.at[i],
            recv_sem=meta_recv.at[i],
            device_id={"query": 1 - core},
        )
        for i, (src, dst) in enumerate(
            [(owner_hbm, owner_v), (block_hbm, block_v), (pattern_hbm, pattern_v), (slot_hbm, slot_v)]
        )
    ]
    for copy in metas:
        copy.start()
    own_meta = [
        pltpu.make_async_copy(src, dst.at[0], smem_sem.at[i])
        for i, (src, dst) in enumerate(
            [(owner_hbm, owner_s), (block_hbm, block_s), (pattern_hbm, pattern_s), (slot_hbm, slot_s)]
        )
    ]
    for copy in own_meta:
        copy.start()

    load_blocks.wait()

    @pl.loop(0, stored)
    def _(b):
        wide = blocks[b].astype(jnp.float32)
        mean = jnp.sum(wide * wide, axis=1, keepdims=True) * (1.0 / depth)
        inverse = lax.rsqrt(mean + 1e-06) * (1.0 / math.sqrt(depth))
        scale[b] = jnp.broadcast_to(inverse, (width, SUB))

    def best_copy(slot, first, count):
        tile = (slot // ny) * ny + lax.rem(slot + y, ny)
        return pltpu.make_async_remote_copy(
            src_ref=best_out.at[pl.ds(slot * subs + first, count)],
            dst_ref=best_in.at[pl.ds(me * subs + first, count)],
            send_sem=best_send.at[slot],
            recv_sem=best_recv.at[me],
            device_id={"store": tile},
        )

    def score(place, unit):
        start = pl.multiple_of(place * ny * rows + unit * UNIT, UNIT)
        column = (place * ny * rows) // SUB + unit * (UNIT // SUB)

        @pl.loop(0, stored // group)
        def _(g):
            first = pl.multiple_of(g * group, group)
            picked = blocks[pl.ds(first, group)].reshape(group * width, depth)
            products = lax.dot_general(
                picked,
                gathered[pl.ds(start, UNIT)],
                (((1,), (1,)), ((), ())),
                preferred_element_type=jnp.float32,
            ).reshape(group, width, UNIT)
            factor = scale[pl.ds(first, group)]
            for j in range(UNIT // SUB):
                piece = products[:, :, j * SUB : (j + 1) * SUB] * factor
                best_out[column + j, pl.ds(first, group)] = jnp.max(piece, axis=1)

    def score_and_send(place, unit):
        score(place, unit)
        slot = place * ny
        if unit == 0:
            @pl.when(place != z)
            def _():
                best_copy(slot, 0, 2).start()
        elif unit == 1:
            @pl.when(place != z)
            def _():
                best_copy(slot, 2, 1).start()

            best_copy(slot + 1, 0, 1).start()
        else:
            best_copy(slot + 1, 1, 2).start()

    def each_side(distance, act):
        @pl.loop(0, 2)
        def _(side):
            place = z + (1 - 2 * side) * distance

            @pl.when((place >= 0) & (place < nz) & ((distance > 0) | (side == 0)))
            def _():
                act(place)

    def spread(place, slot, c):
        @pl.when((place >= z) & (z > 0))
        def _():
            copy_of(slot, c, DOWN).start()

        @pl.when((place <= z) & (z < nz - 1))
        def _():
            copy_of(slot, c, UP).start()

    def pass_line(distance, which):
        for c in which:
            def act(place):
                wait_chunk(place * ny, c)
                spread(place, place * ny, c)
                if c < last:
                    copy_of(place * ny, c, ACROSS).start()

            each_side(distance, act)

    def pass_second(distance):
        def act(place):
            wait_chunk(place * ny + 1, last)
            spread(place, place * ny + 1, last)

        each_side(distance, act)

    def across_unit(distance, unit):
        def act(place):
            for c in (0, 1) if unit == 1 else (2, 3, 4):
                wait_chunk(place * ny + 1, c)
            score_and_send(place, unit)

        each_side(distance, act)

    load_own.wait()
    score_and_send(z, 0)

    @pl.loop(1, nz)
    def _(distance):
        pass_second(distance - 1)
        pass_line(distance, (0,))
        across_unit(distance - 1, 1)
        pass_line(distance, (1, 2))
        across_unit(distance - 1, 2)
        pass_line(distance, (3,))
        each_side(distance, lambda place: score_and_send(place, 0))
        pass_line(distance, (4, 5))

    across_unit(nz - 1, 1)
    pass_second(nz - 1)
    across_unit(nz - 1, 2)
    keep = pltpu.make_async_copy(
        best_out.at[pl.ds(mine * subs, subs)], best_in.at[pl.ds(me * subs, subs)], local_sem.at[0]
    )
    keep.start()

    for copy in metas:
        copy.wait()
    for copy in own_meta:
        copy.wait()
    other_meta = [
        pltpu.make_async_copy(src, dst.at[1], smem_sem.at[i])
        for i, (src, dst) in enumerate(
            [(owner_v, owner_s), (block_v, block_s), (pattern_v, pattern_s), (slot_v, slot_s)]
        )
    ]
    for copy in other_meta:
        copy.start()
    for copy in other_meta:
        copy.wait()

    keep.wait()

    @pl.loop(1, n)
    def _(step):
        source = lax.rem(me + step, n)
        pltpu.make_async_remote_copy(
            src_ref=best_out.at[pl.ds(source * subs, subs)],
            dst_ref=best_in.at[pl.ds(source * subs, subs)],
            send_sem=best_send.at[source],
            recv_sem=best_recv.at[source],
            device_id={"store": source},
        ).wait_recv()

    length = owner_s.shape[2]
    slots = lax.broadcasted_iota(jnp.int32, (SLOTS, SUB), 0)

    def merge(c, totals):
        totals = list(totals)
        for run in range(2):
            shard, block = owner_s[run, 0, c], block_s[run, 0, c]
            slot = slot_s[run, 0, c]
            for j in range(subs):
                live = pattern_s[run, 0, c, core * subs + j] == 1
                wanted = jnp.where(live, slot, -1)
                row = best_in[shard * subs + j, pl.ds(block, 1), :]
                piece = jnp.broadcast_to(row, (SLOTS, SUB))
                totals[j] = jnp.maximum(totals[j], jnp.where(slots == wanted, piece, 0.0))
        return tuple(totals)

    zero = jnp.zeros((SLOTS, SUB), jnp.float32)
    totals = lax.fori_loop(0, length, merge, (zero,) * subs)
    for j in range(subs):
        out_ref[0, :, j * SUB : (j + 1) * SUB] = totals[j]

    for c in range(last + 1):
        copy_of(mine, c, ACROSS, True).wait_send()

    @pl.loop(0, nz)
    def _(place):
        slot = place * ny

        @pl.when(place != z)
        def _():
            for c in range(last):
                copy_of(slot, c, ACROSS).wait_send()

        @pl.when((place <= z) & (z < nz - 1))
        def _():
            for c in range(last + 1):
                copy_of(slot, c, UP).wait_send()
            copy_of(slot + 1, last, UP).wait_send()

        @pl.when((place >= z) & (z > 0))
        def _():
            for c in range(last + 1):
                copy_of(slot, c, DOWN).wait_send()
            copy_of(slot + 1, last, DOWN).wait_send()

    @pl.loop(1, n)
    def _(step):
        best_copy(lax.rem(mine + step, n), 0, subs).wait_send()


def body(queries, store_blocks, cand_owner, cand_block, pattern, slot_index):
    n = lax.axis_size("store")
    rows, depth = queries.shape[1:]
    stored, width = store_blocks.shape[:2]
    length, subs = pattern.shape[1:]
    flat = (1, length)
    return pl.pallas_call(
        functools.partial(kernel, n, 16),
        out_shape=jax.ShapeDtypeStruct((1, SLOTS, rows), jnp.float32),
        in_specs=[pl.BlockSpec(memory_space=pl.ANY)] * 6,
        out_specs=pl.BlockSpec(memory_space=pltpu.VMEM),
        scratch_shapes=[
            pltpu.VMEM((stored, width, depth), jnp.bfloat16),
            pltpu.VMEM((n * rows, depth), jnp.bfloat16),
            pltpu.VMEM((stored, width, SUB), jnp.float32),
            pltpu.VMEM((n * rows // SUB, stored, SUB), jnp.float32),
            pltpu.VMEM((n * rows // SUB, stored, SUB), jnp.float32),
            pltpu.VMEM(flat, jnp.int32),
            pltpu.VMEM(flat, jnp.int32),
            pltpu.VMEM((1, length, subs), jnp.int32),
            pltpu.VMEM(flat, jnp.int32),
            pltpu.SMEM((2,) + flat, jnp.int32),
            pltpu.SMEM((2,) + flat, jnp.int32),
            pltpu.SMEM((2, 1, length, subs), jnp.int32),
            pltpu.SMEM((2,) + flat, jnp.int32),
            pltpu.SemaphoreType.DMA((2,)),
            pltpu.SemaphoreType.DMA((n, CHUNKS)),
            pltpu.SemaphoreType.DMA((3, n, CHUNKS)),
            pltpu.SemaphoreType.DMA((n,)),
            pltpu.SemaphoreType.DMA((n,)),
            pltpu.SemaphoreType.DMA((4,)),
            pltpu.SemaphoreType.DMA((4,)),
            pltpu.SemaphoreType.DMA((4,)),
        ],
        compiler_params=pltpu.CompilerParams(
            collective_id=0, has_side_effects=True, vmem_limit_bytes=60 * MIB
        ),
        cost_estimate=pl.CostEstimate(
            flops=2 * n * rows * stored * width * depth,
            bytes_accessed=stored * width * depth * 2,
            transcendentals=0,
        ),
    )(queries, store_blocks, cand_owner, cand_block, pattern, slot_index)


def solution(mesh):
    placed = (
        P(("parts", "store"), "query", None),
        P(("parts", "store"), None, None),
        P(("parts", "store"), "query"),
        P(("parts", "store"), "query"),
        P(("parts", "store"), "query", None),
        P(("parts", "store"), "query"),
    )
    return jax.shard_map(
        body,
        mesh=mesh,
        in_specs=placed,
        out_specs=P(("parts", "store"), None, "query"),
        check_vma=False,
    )
```

time: 98.7 us -> 87.5 us (0.89)
  Pallas kernels: 94 us -> 84.5 us
  local copies, waits for them, and re-layouts: 4.49 us -> 2.8 us
    pallas_call x1, Pallas kernels: 94 us -> 84.5 us  [body(): pl.pallas_call(functools.partial(kernel, n, 16), out_shape=jax.ShapeDtype...]
    unnamed x10 -> x2, local copies, waits for them, and re-layouts: 4.49 us -> 2.8 us
where the time goes in v2:
time: 87.5 us; the launch traced here: 87.3 us
  Pallas kernels  84.5 us (97%)
  local copies, waits for them, and re-layouts  2.8 us (3%)
    pallas_call x1, Pallas kernels, body(): pl.pallas_call(functools.partial(kernel, n, 16), out_shape=jax.ShapeDtype...  84.5 us
    unnamed x2, local copies, waits for them, and re-layouts  2.8 us

profile of v2, /device:TPU:0, one launch (start us, length us, event | category | flops | bytes accessed | tf_op | source)
XLA Modules:
  0.0 87.3 jit_solution(5543843525906264099)
XLA Ops:
  0.0 1.4 %copy.7.pattern_hbm = s32[1,56,6]{2,1,0:T(8,128)} copy(s32[1,56,6]{1,0,2:T(1,128)} %param.10) | data formatting | bytes 2688 | tf_op args[4]
  1.4 84.5 %shard_map.64 = f32[1,32,384]{2,1,0:T(8,128)} custom-call(bf16[1,384,1024]{2,1,0:T(8,128)(2,1)} %q_hbm.1, bf16[32,128,1024]{2,1,0:T(8,128)(2,1)} %blocks_hbm.1, s32[1,56]{1,0:T(1,128)} %owner_hbm.1, s32[1,56]{1,0:T(1,128)} %block_hbm.1, s32[1,56,6]{2,1,0:T(8,128)} %copy.7.pattern_hbm, s32[1,56]{1,0:T(1,128)} %slot_hbm.1), custom_call_target="tpu_custom_call" | custom-call | flops 25769803776 | bytes 8388608 | tf_op jit(solution)/shard_map/pallas_call | solution.py:342
  85.9 1.4 %copy.9 = f32[1,32,384]{2,1,0:T(8,128)} copy(f32[1,32,384]{2,1,0:T(8,128)} %shard_map.64) | data formatting | bytes 98304

commit v3 on v2

--- a/solution.py
+++ b/solution.py
@@ -52,7 +52,8 @@
     ny = 2
     nz = n // ny
     rows = gathered.shape[0] // n
-    piece_rows = rows // CHUNKS
+    small = rows // 6
+    sizes = [small] * (CHUNKS - 2) + [2 * small - rows // 8, rows // 8]
     subs = rows // SUB
     stored, width, depth = blocks.shape
     last = CHUNKS - 1
@@ -65,8 +66,8 @@
     mine = z * ny
 
     def rows_of(slot, c, count=1):
-        start = pl.multiple_of(slot * rows + c * piece_rows, piece_rows)
-        return gathered.at[pl.ds(start, count * piece_rows)]
+        start = pl.multiple_of(slot * rows + c * small if c < last else (slot + 1) * rows - sizes[last], 16)
+        return gathered.at[pl.ds(start, sum(sizes[c : c + count]))]
 
     load_blocks = pltpu.make_async_copy(blocks_hbm, blocks, local_sem.at[0])
     load_blocks.start()
@@ -89,7 +90,7 @@
     )
 
     def copy_of(slot, c, way, own=False):
-        source = q_hbm.at[0, pl.ds(c * piece_rows, piece_rows)] if own else rows_of(slot, c)
+        source = q_hbm.at[0, pl.ds(sum(sizes[:c]), sizes[c])] if own else rows_of(slot, c)
         landing = slot + 1 if way == ACROSS else slot
         return pltpu.make_async_remote_copy(
             src_ref=source,
@@ -235,6 +236,18 @@
 
     load_own.wait()
     score_and_send(z, 0)
+    for copy in metas:
+        copy.wait()
+    for copy in own_meta:
+        copy.wait()
+    other_meta = [
+        pltpu.make_async_copy(src, dst.at[1], smem_sem.at[i])
+        for i, (src, dst) in enumerate(
+            [(owner_v, owner_s), (block_v, block_s), (pattern_v, pattern_s), (slot_v, slot_s)]
+        )
+    ]
+    for copy in other_meta:
+        copy.start()
 
     @pl.loop(1, nz)
     def _(distance):
@@ -255,20 +268,32 @@
     )
     keep.start()
 
-    for copy in metas:
-        copy.wait()
-    for copy in own_meta:
-        copy.wait()
-    other_meta = [
-        pltpu.make_async_copy(src, dst.at[1], smem_sem.at[i])
-        for i, (src, dst) in enumerate(
-            [(owner_v, owner_s), (block_v, block_s), (pattern_v, pattern_s), (slot_v, slot_s)]
-        )
-    ]
-    for copy in other_meta:
-        copy.start()
     for copy in other_meta:
         copy.wait()
+
+    for c in range(last + 1):
+        copy_of(mine, c, ACROSS, True).wait_send()
+
+    @pl.loop(0, nz)
+    def _(place):
+        slot = place * ny
+
+        @pl.when(place != z)
+        def _():
+            for c in range(last):
+                copy_of(slot, c, ACROSS).wait_send()
+
+        @pl.when((place <= z) & (z < nz - 1))
+        def _():
+            for c in range(last + 1):
+                copy_of(slot, c, UP).wait_send()
+            copy_of(slot + 1, last, UP).wait_send()
+
+        @pl.when((place >= z) & (z > 0))
+        def _():
+            for c in range(last + 1):
+                copy_of(slot, c, DOWN).wait_send()
+            copy_of(slot + 1, last, DOWN).wait_send()
 
     keep.wait()
 
@@ -292,7 +317,7 @@
             shard, block = owner_s[run, 0, c], block_s[run, 0, c]
             slot = slot_s[run, 0, c]
             for j in range(subs):
-                live = pattern_s[run, 0, c, core * subs + j] == 1
+                live = pattern_s[run, core * subs + j, 0, c] == 1
                 wanted = jnp.where(live, slot, -1)
                 row = best_in[shard * subs + j, pl.ds(block, 1), :]
                 piece = jnp.broadcast_to(row, (SLOTS, SUB))
@@ -300,33 +325,9 @@
         return tuple(totals)
 
     zero = jnp.zeros((SLOTS, SUB), jnp.float32)
-    totals = lax.fori_loop(0, length, merge, (zero,) * subs)
+    totals = lax.fori_loop(0, length, merge, (zero,) * subs, unroll=8)
     for j in range(subs):
         out_ref[0, :, j * SUB : (j + 1) * SUB] = totals[j]
-
-    for c in range(last + 1):
-        copy_of(mine, c, ACROSS, True).wait_send()
-
-    @pl.loop(0, nz)
-    def _(place):
-        slot = place * ny
-
-        @pl.when(place != z)
-        def _():
-            for c in range(last):
-                copy_of(slot, c, ACROSS).wait_send()
-
-        @pl.when((place <= z) & (z < nz - 1))
-        def _():
-            for c in range(last + 1):
-                copy_of(slot, c, UP).wait_send()
-            copy_of(slot + 1, last, UP).wait_send()
-
-        @pl.when((place >= z) & (z > 0))
-        def _():
-            for c in range(last + 1):
-                copy_of(slot, c, DOWN).wait_send()
-            copy_of(slot + 1, last, DOWN).wait_send()
 
     @pl.loop(1, n)
     def _(step):
@@ -340,7 +341,7 @@
     length, subs = pattern.shape[1:]
     flat = (1, length)
     return pl.pallas_call(
-        functools.partial(kernel, n, 16),
+        functools.partial(kernel, n, 32),
         out_shape=jax.ShapeDtypeStruct((1, SLOTS, rows), jnp.float32),
         in_specs=[pl.BlockSpec(memory_space=pl.ANY)] * 6,
         out_specs=pl.BlockSpec(memory_space=pltpu.VMEM),
@@ -352,11 +353,11 @@
             pltpu.VMEM((n * rows // SUB, stored, SUB), jnp.float32),
             pltpu.VMEM(flat, jnp.int32),
             pltpu.VMEM(flat, jnp.int32),
-            pltpu.VMEM((1, length, subs), jnp.int32),
+            pltpu.VMEM((subs, 1, length), jnp.int32),
             pltpu.VMEM(flat, jnp.int32),
             pltpu.SMEM((2,) + flat, jnp.int32),
             pltpu.SMEM((2,) + flat, jnp.int32),
-            pltpu.SMEM((2, 1, length, subs), jnp.int32),
+            pltpu.SMEM((2, subs, 1, length), jnp.int32),
             pltpu.SMEM((2,) + flat, jnp.int32),
             pltpu.SemaphoreType.DMA((2,)),
             pltpu.SemaphoreType.DMA((n, CHUNKS)),
@@ -375,7 +376,7 @@
             bytes_accessed=stored * width * depth * 2,
             transcendentals=0,
         ),
-    )(queries, store_blocks, cand_owner, cand_block, pattern, slot_index)
+    )(queries, store_blocks, cand_owner, cand_block, pattern.transpose(2, 0, 1), slot_index)
 
 
 def solution(mesh):

time: 87.5 us -> 85.8 us (0.981)
  local copies, waits for them, and re-layouts: 2.8 us -> 1.42 us
    unnamed x2 -> x1, local copies, waits for them, and re-layouts: 2.8 us -> 1.42 us
where the time goes in v3:
time: 85.8 us; the launch traced here: 85.6 us
  Pallas kernels  84.2 us (98%)
  local copies, waits for them, and re-layouts  1.42 us (2%)
    pallas_call x1, Pallas kernels, body(): pl.pallas_call(functools.partial(kernel, n, 32), out_shape=jax.ShapeDtype...  84.2 us

profile of v3, /device:TPU:0, one launch (start us, length us, event | category | flops | bytes accessed | tf_op | source)
XLA Modules:
  0.0 85.6 jit_solution(15315986035624597210)
XLA Ops:
  0.0 84.2 %shard_map.64 = f32[1,32,384]{2,1,0:T(8,128)} custom-call(bf16[1,384,1024]{2,1,0:T(8,128)(2,1)} %q_hbm.1, bf16[32,128,1024]{2,1,0:T(8,128)(2,1)} %blocks_hbm.1, s32[1,56]{1,0:T(1,128)} %owner_hbm.1, s32[1,56]{1,0:T(1,128)} %block_hbm.1, s32[6,1,56]{2,1,0:T(1,128)} %bitcast.1, s32[1,56]{1,0:T(1,128)} %slot_hbm.1), custom_call_target="tpu_custom_call" | custom-call | flops 25769803776 | bytes 8388608 | tf_op jit(solution)/shard_map/pallas_call | solution.py:343
  84.2 1.4 %copy.8 = f32[1,32,384]{2,1,0:T(8,128)} copy(f32[1,32,384]{2,1,0:T(8,128)} %shard_map.64) | data formatting | bytes 98304

commit v4 on v3

--- a/solution.py
+++ b/solution.py
@@ -53,7 +53,7 @@
     nz = n // ny
     rows = gathered.shape[0] // n
     small = rows // 6
-    sizes = [small] * (CHUNKS - 2) + [2 * small - rows // 8, rows // 8]
+    sizes = [small] * (CHUNKS - 2) + [2 * small - rows // 6, rows // 6]
     subs = rows // SUB
     stored, width, depth = blocks.shape
     last = CHUNKS - 1
@@ -252,11 +252,10 @@
     @pl.loop(1, nz)
     def _(distance):
         pass_second(distance - 1)
-        pass_line(distance, (0,))
+        pass_line(distance, (0, 1))
         across_unit(distance - 1, 1)
-        pass_line(distance, (1, 2))
+        pass_line(distance, (2, 3))
         across_unit(distance - 1, 2)
-        pass_line(distance, (3,))
         each_side(distance, lambda place: score_and_send(place, 0))
         pass_line(distance, (4, 5))
 

time: 85.8 us -> 83.4 us (0.972)
  Pallas kernels: 84.2 us -> 81.8 us
    pallas_call x1, Pallas kernels: 84.2 us -> 81.8 us  [body(): pl.pallas_call(functools.partial(kernel, n, 32), out_shape=jax.ShapeDtype...]
where the time goes in v4:
time: 83.4 us; the launch traced here: 83.3 us
  Pallas kernels  81.8 us (98%)
  local copies, waits for them, and re-layouts  1.42 us (2%)
    pallas_call x1, Pallas kernels, body(): pl.pallas_call(functools.partial(kernel, n, 32), out_shape=jax.ShapeDtype...  81.8 us

profile of v4, /device:TPU:0, one launch (start us, length us, event | category | flops | bytes accessed | tf_op | source)
XLA Modules:
  0.0 83.3 jit_solution(5467460325357602172)
XLA Ops:
  0.0 81.8 %shard_map.64 = f32[1,32,384]{2,1,0:T(8,128)} custom-call(bf16[1,384,1024]{2,1,0:T(8,128)(2,1)} %q_hbm.1, bf16[32,128,1024]{2,1,0:T(8,128)(2,1)} %blocks_hbm.1, s32[1,56]{1,0:T(1,128)} %owner_hbm.1, s32[1,56]{1,0:T(1,128)} %block_hbm.1, s32[6,1,56]{2,1,0:T(1,128)} %bitcast.1, s32[1,56]{1,0:T(1,128)} %slot_hbm.1), custom_call_target="tpu_custom_call" | custom-call | flops 25769803776 | bytes 8388608 | tf_op jit(solution)/shard_map/pallas_call | solution.py:342
  81.8 1.4 %copy.8 = f32[1,32,384]{2,1,0:T(8,128)} copy(f32[1,32,384]{2,1,0:T(8,128)} %shard_map.64) | data formatting | bytes 98304
